TPU v7x, 32 devices: a whole 2x2x4 slice. The times are simulated.
32 devices in a mesh: fsdp: 2 (over x), ctx: 16 (over z, y, core).
Axes of the slice: x: 2, y: 2, z: 4, core: 2. Of those that a mesh axis runs over, the one named last changes fastest.
Arguments:
- tokens: bfloat16 [8192, 1024], P(('fsdp', 'ctx')), may hold values from -6 to 6
- block_pairs: int32 [16], replicated, may hold values from 0 to 15, each once
- norm_gain: bfloat16 [1024], P('fsdp'), may hold values from 0.5 to 1.5
- norm_bias: bfloat16 [1024], P('fsdp'), may hold values from -4 to 4
- qkv_weight: bfloat16 [1024, 3072], P(None, 'fsdp'), may hold values from -0.1875 to 0.1875
- out_weight: bfloat16 [1024, 1024], P('fsdp'), may hold values from -3 to 3
- up_weight: bfloat16 [1024, 4096], P(None, 'fsdp'), may hold values from -0.1875 to 0.1875
- up_bias: bfloat16 [4096], P('fsdp'), may hold values from -6 to 6
- down_weight: bfloat16 [4096, 1024], P('fsdp'), may hold values from -0.09375 to 0.09375
- down_bias: bfloat16 [1024], P('fsdp'), may hold values from -4 to 4
- cotangent: bfloat16 [8192, 1024], P(('fsdp', 'ctx')), may hold values from -6 to 6
Outputs:
- mixed: bfloat16 [8192, 1024], P(('fsdp', 'ctx'))
- tokens_grad: bfloat16 [8192, 1024], P(('fsdp', 'ctx'))
- norm_gain_grad: float32 [1024], P('fsdp')
- norm_bias_grad: float32 [1024], P('fsdp')
- qkv_weight_grad: float32 [1024, 3072], P(None, 'fsdp')
- out_weight_grad: float32 [1024, 1024], P('fsdp')
- up_weight_grad: float32 [1024, 4096], P(None, 'fsdp')
- up_bias_grad: float32 [4096], P('fsdp')
- down_weight_grad: float32 [4096, 1024], P('fsdp')
- down_bias_grad: float32 [1024], P('fsdp')
Inputs may be any that keep to these rules, and one draw needn't show every extreme that they name: a permutation: each ctx device holds block block_pairs[c] and its mirror 2 * (number of ctx devices) - 1 - block_pairs[c] of every sequence.
All inputs are finite; a program needn't handle non-finite values.
Results may differ from a plain program's by a relative error of at most 0.012.
Values may be sent and summed in bfloat16 or wider, within the bound.
A program may use at most 576 MiB of HBM per device.

v0:
```python
import math

import jax
import jax.numpy as jnp
from jax import lax
from jax.sharding import PartitionSpec as P

D = 1024
HEAD_DIM = 64
ROT_DIM = 32
HEADS = 16
SEQ_DEV_TOK = 128
SEQS = 2


EPS = 1e-05
HIGHEST = lax.Precision.HIGHEST
masked_score = -1e30


def layer_norm(values, gain_values, shift_values):
    center = values - jnp.mean(values, axis=-1, keepdims=True)
    spread = jnp.mean(center * center, axis=-1, keepdims=True)
    return center * lax.rsqrt(spread + EPS) * gain_values + shift_values


def rotary_tables(places, window):
    lanes = jnp.arange(window, dtype=jnp.int32)
    within_head = lanes % HEAD_DIM
    turning = within_head < ROT_DIM
    steps_up = (within_head // 2 * 2).astype(jnp.float32)
    speeds = 10000.0 ** (-steps_up / ROT_DIM)
    phase = places.astype(jnp.float32)[:, None] * speeds[None, :]
    cos_full = jnp.where(turning[None, :], jnp.cos(phase), 1.0)
    sin_full = jnp.where(turning[None, :], jnp.sin(phase), 0.0)
    row_lane = lanes[:, None]
    col_lane = lanes[None, :]
    same_head = row_lane // HEAD_DIM == col_lane // HEAD_DIM
    col_within = col_lane % HEAD_DIM
    col_turns = same_head & (col_within < ROT_DIM)
    even_col = col_within % 2 == 0
    minus_part = jnp.where(col_turns & even_col & (row_lane == col_lane + 1), -1.0, 0.0)
    plus_part = jnp.where(
        col_turns & jnp.logical_not(even_col) & (row_lane == col_lane - 1), 1.0, 0.0
    )
    swap_table = (minus_part + plus_part).astype(jnp.float32)
    return (cos_full, sin_full, swap_table)


def smooth_gate(values):
    return jax.nn.gelu(values, approximate=True)


def positions(first_row, row_count, pair_table, devices, seq_rows):
    indices = first_row + jnp.arange(row_count, dtype=jnp.int32)
    owners = indices // seq_rows
    within = indices % seq_rows
    half_rows = seq_rows // 2
    matches = owners[:, None] == jnp.arange(devices, dtype=jnp.int32)[None, :]
    chosen = jnp.sum(jnp.where(matches, pair_table[None, :], 0), axis=1)
    block_index = jnp.where(within < half_rows, chosen, 2 * devices - 1 - chosen)
    return block_index * half_rows + within % half_rows


def in_groups(row_count, seq_rows):
    group_rows = math.gcd(row_count // seq_rows, 8) * seq_rows
    return (group_rows, row_count // group_rows)


def split_groups(array, group_rows, turns):
    return array.reshape((turns, group_rows) + array.shape[1:])


def grad_scores(
    query_rows,
    out_grads,
    log_sums,
    row_dots,
    query_places,
    key_rows,
    value_rows,
    key_places,
    factor,
):
    scores = (
        jnp.einsum("qshe,kshe->shqk", query_rows, key_rows, preferred_element_type=jnp.float32)
        * factor
    )
    allowed = key_places[None, :] <= query_places[:, None]
    chances = jnp.exp(jnp.where(allowed, scores - log_sums[..., None], masked_score))
    prob_grads = jnp.einsum(
        "qshe,kshe->shqk", out_grads, value_rows, preferred_element_type=jnp.float32
    )
    return (chances, (chances * (prob_grads - row_dots[..., None])).astype(jnp.bfloat16))


def per_device(
    tokens,
    block_pairs,
    norm_gain,
    norm_bias,
    qkv_weight,
    out_weight,
    up_weight,
    up_bias,
    down_weight,
    down_bias,
    cotangent,
):
    devices = lax.axis_size("ctx")
    own_index = lax.axis_index("ctx")
    seq_rows = SEQ_DEV_TOK
    seq_count = SEQS
    heads = HEADS
    head_size = HEAD_DIM
    width = D
    factor = HEAD_DIM ** (-0.5)
    all_rows = seq_rows * seq_count
    window = math.gcd(width, 128)
    gathered = (
        lax.all_gather(norm_gain, "fsdp", axis=0, tiled=True),
        lax.all_gather(norm_bias, "fsdp", axis=0, tiled=True),
        lax.all_gather(qkv_weight, "fsdp", axis=1, tiled=True),
        lax.all_gather(out_weight, "fsdp", axis=0, tiled=True),
        lax.all_gather(up_weight, "fsdp", axis=1, tiled=True),
        lax.all_gather(up_bias, "fsdp", axis=0, tiled=True),
        lax.all_gather(down_weight, "fsdp", axis=0, tiled=True),
        lax.all_gather(down_bias, "fsdp", axis=0, tiled=True),
    )
    gain_low, shift_low, w_qkv, w_out, w_up, b_up, w_down, b_down = gathered
    inputs = tokens.astype(jnp.float32)
    gain_values = gain_low.astype(jnp.float32)
    shift_values = shift_low.astype(jnp.float32)
    normed_low = layer_norm(inputs, gain_values, shift_values).astype(jnp.bfloat16)
    mixed_qkv = jnp.dot(normed_low, w_qkv, preferred_element_type=jnp.float32).reshape(
        seq_rows, seq_count, 3 * width
    )
    own_places = positions(own_index * seq_rows, seq_rows, block_pairs, devices, seq_rows)
    cos_full, sin_full, swap_table = rotary_tables(own_places, window)

    def turn_both(values):
        shaped = values.reshape(seq_rows, seq_count, 2 * width // window, window)
        swapped = jnp.einsum("rsgw,wv->rsgv", shaped, swap_table, precision=HIGHEST)
        turned_rows = shaped * cos_full[:, None, None, :] + swapped * sin_full[:, None, None, :]
        return turned_rows.reshape(seq_rows, seq_count, 2 * width)

    query_key = mixed_qkv[:, :, : 2 * width]
    turned = turn_both(query_key)
    queries = (
        turned[:, :, :width].astype(jnp.bfloat16).reshape(seq_rows, seq_count, heads, head_size)
    )
    key_rows = (
        turned[:, :, width:].astype(jnp.bfloat16).reshape(seq_rows, seq_count, heads, head_size)
    )
    value_rows = (
        mixed_qkv[:, :, 2 * width :]
        .astype(jnp.bfloat16)
        .reshape(seq_rows, seq_count, heads, head_size)
    )
    start_state = (
        jnp.full((seq_count, heads, seq_rows), masked_score, jnp.float32),
        jnp.zeros((seq_count, heads, seq_rows), jnp.float32),
        jnp.zeros((seq_count, heads, seq_rows, head_size), jnp.float32),
    )
    piece_keys = lax.all_gather(key_rows, "ctx", axis=0, tiled=True)
    piece_values = lax.all_gather(value_rows, "ctx", axis=0, tiled=True)
    group_rows, turns = in_groups(piece_keys.shape[0], seq_rows)

    def attend_step(inner, item):
        block_keys, block_values, turn = item
        key_places = positions(turn * group_rows, group_rows, block_pairs, devices, seq_rows)
        scores = (
            jnp.einsum("qshe,kshe->shqk", queries, block_keys, preferred_element_type=jnp.float32)
            * factor
        )
        allowed = key_places[None, :] <= own_places[:, None]
        running, totals, accum = inner
        fresh = jnp.maximum(running, jnp.max(jnp.where(allowed, scores, masked_score), axis=-1))
        weights = jnp.exp(jnp.where(allowed, scores - fresh[..., None], masked_score))
        fading = jnp.exp(running - fresh)
        totals = totals * fading + jnp.sum(weights, axis=-1)
        accum = accum * fading[..., None] + jnp.einsum(
            "shqk,kshe->shqe",
            weights.astype(jnp.bfloat16),
            block_values,
            preferred_element_type=jnp.float32,
        )
        return ((fresh, totals, accum), None)

    inner, _ = lax.scan(
        attend_step,
        start_state,
        (
            split_groups(piece_keys, group_rows, turns),
            split_groups(piece_values, group_rows, turns),
            jnp.arange(turns, dtype=jnp.int32),
        ),
    )
    running, totals, accum = inner
    log_sums = running + jnp.log(totals)
    attended = jnp.transpose(accum / totals[..., None], (2, 0, 1, 3))
    attn_low = attended.reshape(all_rows, width).astype(jnp.bfloat16)
    attention = jnp.dot(attn_low, w_out, preferred_element_type=jnp.float32)
    up_pre = jnp.dot(normed_low, w_up, preferred_element_type=jnp.float32) + b_up.astype(
        jnp.float32
    )
    hidden_low = smooth_gate(up_pre).astype(jnp.bfloat16)
    result = (
        inputs
        + attention
        + jnp.dot(hidden_low, w_down, preferred_element_type=jnp.float32)
        + b_down.astype(jnp.float32)
    )
    mixed = result.astype(jnp.bfloat16)
    again = (
        lax.all_gather(norm_gain, "fsdp", axis=0, tiled=True),
        lax.all_gather(norm_bias, "fsdp", axis=0, tiled=True),
        lax.all_gather(qkv_weight, "fsdp", axis=1, tiled=True),
        lax.all_gather(out_weight, "fsdp", axis=0, tiled=True),
        lax.all_gather(up_weight, "fsdp", axis=1, tiled=True),
        lax.all_gather(up_bias, "fsdp", axis=0, tiled=True),
        lax.all_gather(down_weight, "fsdp", axis=0, tiled=True),
        lax.all_gather(down_bias, "fsdp", axis=0, tiled=True),
    )
    gain_low, shift_low, w_qkv, w_out, w_up, b_up, w_down, b_down = again
    out_grad = cotangent.astype(jnp.float32)
    attn_grads = (
        jnp.einsum("td,ed->te", cotangent, w_out, preferred_element_type=jnp.float32)
        .astype(jnp.bfloat16)
        .reshape(seq_rows, seq_count, heads, head_size)
    )
    dots_rows = jnp.sum(attn_grads.astype(jnp.float32) * attended, axis=-1)
    row_dots = jnp.transpose(dots_rows, (1, 2, 0))
    empty_rows = jnp.zeros((seq_rows, seq_count, heads, head_size), jnp.float32)
    whole_keys, whole_values = (
        lax.all_gather(key_rows, "ctx", axis=0, tiled=True),
        lax.all_gather(value_rows, "ctx", axis=0, tiled=True),
    )
    piece_keys = whole_keys
    piece_values = whole_values
    query_group_rows, turns = in_groups(piece_keys.shape[0], seq_rows)

    def query_step(inner, item):
        block_keys, block_values, turn = item
        key_places = positions(
            0 + turn * query_group_rows, query_group_rows, block_pairs, devices, seq_rows
        )
        chances, score_grads = grad_scores(
            queries,
            attn_grads,
            log_sums,
            row_dots,
            own_places,
            block_keys,
            block_values,
            key_places,
            factor,
        )
        return (
            inner
            + jnp.einsum(
                "shqk,kshe->qshe", score_grads, block_keys, preferred_element_type=jnp.float32
            )
            * factor,
            None,
        )

    inner, _ = lax.scan(
        query_step,
        empty_rows,
        (
            split_groups(piece_keys, query_group_rows, turns),
            split_groups(piece_values, query_group_rows, turns),
            jnp.arange(turns, dtype=jnp.int32),
        ),
    )
    query_grad = inner
    piece_keys = whole_keys
    piece_values = whole_values
    key_group_rows, turns = in_groups(seq_rows * lax.axis_size("ctx"), seq_rows)

    def key_step(inner, item):
        block_keys, block_values, turn = item
        key_places = positions(
            turn * key_group_rows, key_group_rows, block_pairs, devices, seq_rows
        )
        chances, score_grads = grad_scores(
            queries,
            attn_grads,
            log_sums,
            row_dots,
            own_places,
            block_keys,
            block_values,
            key_places,
            factor,
        )
        key_part = (
            jnp.einsum("shqk,qshe->kshe", score_grads, queries, preferred_element_type=jnp.float32)
            * factor
        )
        value_part = jnp.einsum(
            "shqk,qshe->kshe",
            chances.astype(jnp.bfloat16),
            attn_grads,
            preferred_element_type=jnp.float32,
        )
        stacked = jnp.stack(
            (
                key_part.reshape(key_group_rows, seq_count, width),
                value_part.reshape(key_group_rows, seq_count, width),
            ),
            axis=2,
        )
        return (inner, stacked)

    _, blocks_out = lax.scan(
        key_step,
        jnp.zeros((), jnp.float32),
        (
            split_groups(piece_keys, key_group_rows, turns),
            split_groups(piece_values, key_group_rows, turns),
            jnp.arange(turns, dtype=jnp.int32),
        ),
    )
    summed_terms = lax.psum_scatter(
        blocks_out.reshape(seq_rows * lax.axis_size("ctx"), seq_count, 2, width),
        "ctx",
        scatter_dimension=0,
        tiled=True,
    )
    key_grad = summed_terms[:, :, 0].reshape(seq_rows, seq_count, heads, head_size)
    value_grad = summed_terms[:, :, 1].reshape(seq_rows, seq_count, heads, head_size)
    _, turn_back = jax.vjp(turn_both, query_key)
    both_grads = jnp.concatenate(
        (
            query_grad.reshape(seq_rows, seq_count, width),
            key_grad.reshape(seq_rows, seq_count, width),
        ),
        axis=2,
    )
    (pre_grads,) = turn_back(both_grads)
    qkv_grad = (
        jnp.concatenate((pre_grads, value_grad.reshape(seq_rows, seq_count, width)), axis=2)
        .reshape(all_rows, 3 * width)
        .astype(jnp.bfloat16)
    )
    hidden_grad = jnp.einsum("td,fd->tf", cotangent, w_down, preferred_element_type=jnp.float32)
    _, gate_back = jax.vjp(smooth_gate, up_pre)
    (up_grad,) = gate_back(hidden_grad)
    up_low = up_grad.astype(jnp.bfloat16)
    normed_grad = jnp.einsum(
        "tc,dc->td", qkv_grad, w_qkv, preferred_element_type=jnp.float32
    ) + jnp.einsum("tf,df->td", up_low, w_up, preferred_element_type=jnp.float32)
    _, norm_back = jax.vjp(
        layer_norm, inputs, gain_low.astype(jnp.float32), shift_low.astype(jnp.float32)
    )
    input_part, gain_grad, shift_grad = norm_back(normed_grad)
    tokens_grad = (out_grad + input_part).astype(jnp.bfloat16)
    qkv_wgrad = jnp.einsum("td,tc->dc", normed_low, qkv_grad, preferred_element_type=jnp.float32)
    out_wgrad = jnp.einsum("td,te->de", attn_low, cotangent, preferred_element_type=jnp.float32)
    up_wgrad = jnp.einsum("td,tf->df", normed_low, up_low, preferred_element_type=jnp.float32)
    up_bgrad = jnp.sum(up_low.astype(jnp.float32), axis=0)
    down_wgrad = jnp.einsum("tf,td->fd", hidden_low, cotangent, preferred_element_type=jnp.float32)
    down_bgrad = jnp.sum(out_grad, axis=0)
    shares = (
        lax.psum_scatter(
            gain_grad.astype(jnp.bfloat16), "fsdp", scatter_dimension=0, tiled=True
        ).astype(jnp.float32),
        lax.psum_scatter(
            shift_grad.astype(jnp.bfloat16), "fsdp", scatter_dimension=0, tiled=True
        ).astype(jnp.float32),
        lax.psum_scatter(
            qkv_wgrad.astype(jnp.bfloat16), "fsdp", scatter_dimension=1, tiled=True
        ).astype(jnp.float32),
        lax.psum_scatter(
            out_wgrad.astype(jnp.bfloat16), "fsdp", scatter_dimension=0, tiled=True
        ).astype(jnp.float32),
        lax.psum_scatter(
            up_wgrad.astype(jnp.bfloat16), "fsdp", scatter_dimension=1, tiled=True
        ).astype(jnp.float32),
        lax.psum_scatter(
            up_bgrad.astype(jnp.bfloat16), "fsdp", scatter_dimension=0, tiled=True
        ).astype(jnp.float32),
        lax.psum_scatter(
            down_wgrad.astype(jnp.bfloat16), "fsdp", scatter_dimension=0, tiled=True
        ).astype(jnp.float32),
        lax.psum_scatter(
            down_bgrad.astype(jnp.bfloat16), "fsdp", scatter_dimension=0, tiled=True
        ).astype(jnp.float32),
    )
    share_gain, share_shift, share_qkv, share_out, share_up, share_upb, share_down, share_downb = (
        shares
    )
    totals_out = lax.psum(
        (
            share_gain,
            share_shift,
            share_qkv,
            share_out,
            share_up,
            share_upb,
            share_down,
            share_downb,
        ),
        "ctx",
    )
    sum_gain, sum_shift, sum_qkv, sum_out, sum_up, sum_upb, sum_down, sum_downb = totals_out
    return (
        mixed,
        tokens_grad,
        sum_gain,
        sum_shift,
        sum_qkv,
        sum_out,
        sum_up,
        sum_upb,
        sum_down,
        sum_downb,
    )


def solution(mesh):
    in_specs = (
        P(("fsdp", "ctx"), None),
        P(),
        P("fsdp"),
        P("fsdp"),
        P(None, "fsdp"),
        P("fsdp", None),
        P(None, "fsdp"),
        P("fsdp"),
        P("fsdp", None),
        P("fsdp"),
        P(("fsdp", "ctx"), None),
    )
    out_specs = (
        P(("fsdp", "ctx"), None),
        P(("fsdp", "ctx"), None),
        P("fsdp"),
        P("fsdp"),
        P(None, "fsdp"),
        P("fsdp", None),
        P(None, "fsdp"),
        P("fsdp"),
        P("fsdp", None),
        P("fsdp"),
    )
    return jax.shard_map(
        per_device, mesh=mesh, in_specs=in_specs, out_specs=out_specs, check_vma=False
    )
```

profile of v0, /device:TPU:9, one launch (start us, length us, event | category | flops | bytes accessed | tf_op | source)
XLA Modules:
  0.0 1727.5 jit_solution(14499532445094162037)
XLA Ops:
  16.5 74.7 %all-gather.10.cloned.1.call-done = bf16[1024,3072]{1,0:T(8,128)(2,1)} async-done(((bf16[1024,1536]{1,0:T(8,128)(2,1)}), bf16[1024,3072]{1,0:T(8,128)(2,1)}) %all-gather.10.cloned.1.call-update) | async-done | bytes 6291472 | tf_op jit(solution)/shard_map/all_gather | solution.py:123
  130.0 75.3 %all-gather.12.cloned.1.call-done = bf16[2048,2,16,64]{0,3,2,1:T(8,128)(2,1)} async-done(((bf16[128,2,16,64]{0,3,2,1:T(8,128)(2,1)}), bf16[2048,2,16,64]{0,3,2,1:T(8,128)(2,1)}) %all-gather.12.cloned.1.call-update) | async-done | bytes 8388624 | tf_op jit(solution)/shard_map/all_gather | solution.py:165
  213.5 70.7 %all-gather.14.cloned.1.call-done = bf16[2048,2,16,64]{0,3,2,1:T(8,128)(2,1)} async-done(((bf16[128,2,16,64]{0,3,2,1:T(8,128)(2,1)}), bf16[2048,2,16,64]{0,3,2,1:T(8,128)(2,1)}) %all-gather.14.cloned.1.call-update) | async-done | bytes 8388624 | tf_op jit(solution)/shard_map/all_gather | solution.py:166
  292.4 80.8 %while.46 = (s32[]{:T(128)}, f32[2,16,128]{2,1,0:T(8,128)S(1)}, f32[2,16,128]{2,1,0:T(8,128)S(1)}, f32[2,16,128,64]{2,3,1,0:T(8,128)}, s32[2]{0:T(128)S(1)}, /*i...) while((s32[]{:T(128)}, f32[2,16,128]{2,1,0:T(8,128)S(1)}, ...), condition=%wide.region_7.8_spmd.clone, body=%wide.region_3.7_spmd.clone.sunk | while | flops 1120910336 | bytes 70543128 | solution.py:190
  294.0 13.0 fusion.260
  380.1 159.7 %while.45 = (s32[]{:T(128)}, f32[2,1024,2,2,1024]{4,1,0,3,2:T(8,128)}, s32[2]{0:T(128)S(1)}, s32[16]{0:T(128)S(1)}, s32[128]{0:T(128)S(1)}, /*index=5*/bf16[2,10...) while((s32[]{:T(128)}, ...), condition=%wide.region_14.15_spmd, body=%wide.region_12.14_spmd.sunk | while | flops 2195942400 | bytes 178727152 | solution.py:317
  392.0 13.9 broadcast_multiply_fusion.3
  406.0 14.5 fusion.255
  420.5 11.8 maximum_bitcast_fusion.2
  432.3 16.4 copy.143
  472.4 13.9 broadcast_multiply_fusion.3
  486.3 13.4 fusion.255
  499.7 11.8 maximum_bitcast_fusion.2
  511.6 16.4 copy.143
  552.7 13.3 fusion.184
  592.9 50.6 %while.47 = (s32[]{:T(128)}, f32[128,2,16,64]{0,3,2,1:T(8,128)}, bf16[2,1024,2,16,64]{1,4,3,2,0:T(8,128)(2,1)}, s32[2]{0:T(128)S(1)}, s32[16]{0:T(128)S(1)}, /*i...) while((s32[]{:T(128)}, f32[128,2,16,64]{0,3,2,1:T(8,128)}, ...), condition=%wide.region_11.12_spmd.clone, body=%wide.region_9.11_spmd.clone.sunk | while | flops 1636789248 | bytes 57993508 | solution.py:268
  604.9 12.0 fusion.272
  630.2 12.3 fusion.272
  643.5 227.8 %reduce-scatter.6.cloned.1.call-done = f32[128,2,2,1024]{3,0,2,1:T(8,128)} async-done(((f32[2048,2,2,1024]{3,0,2,1:T(8,128)}), f32[128,2,2,1024]{3,0,2,1:T(8,128)}) %reduce-scatter.6.cloned.1.call-update) | async-done | bytes 2097168 | tf_op jit(solution)/shard_map/reduce_scatter | solution.py:326
  913.4 59.9 %reduce-scatter.12.cloned.1.call-done = bf16[1024,2048]{1,0:T(8,128)(2,1)} async-done(((bf16[1024,4096]{1,0:T(8,128)(2,1)}), bf16[1024,2048]{1,0:T(8,128)(2,1)}) %reduce-scatter.12.cloned.1.call-update) | async-done | bytes 4194320 | tf_op jit(solution)/shard_map/reduce_scatter | solution.py:379
  973.3 101.7 %reduce-scatter.14.cloned.1.call-done = bf16[2048,1024]{1,0:T(8,128)(2,1)} async-done(((bf16[4096,1024]{1,0:T(8,128)(2,1)}), bf16[2048,1024]{1,0:T(8,128)(2,1)}) %reduce-scatter.14.cloned.1.call-update) | async-done | bytes 4194320 | tf_op jit(solution)/shard_map/reduce_scatter | solution.py:385
  1075.0 34.5 %reduce-scatter.10.cloned.1.call-done = bf16[512,1024]{1,0:T(8,128)(2,1)} async-done(((bf16[1024,1024]{1,0:T(8,128)(2,1)}), bf16[512,1024]{1,0:T(8,128)(2,1)}) %reduce-scatter.10.cloned.1.call-update) | async-done | bytes 1048592 | tf_op jit(solution)/shard_map/reduce_scatter | solution.py:376
  1122.3 67.6 %reduce-scatter.8.cloned.1.call-done = bf16[1024,1536]{1,0:T(8,128)(2,1)} async-done(((bf16[1024,3072]{1,0:T(8,128)(2,1)}), bf16[1024,1536]{1,0:T(8,128)(2,1)}) %reduce-scatter.8.cloned.1.call-update) | async-done | bytes 3145744 | tf_op jit(solution)/shard_map/reduce_scatter | solution.py:373
  1189.9 530.9 %all-reduce.7 = (f32[512]{0:T(512)}, f32[512]{0:T(512)}, f32[1024,1536]{1,0:T(8,128)}, f32[512,1024]{1,0:T(8,128)}, f32[1024,2048]{1,0:T(8,128)}, /*index=5*/f32[2048]{0:T(1024)}, f32[2048,1024]{1,0:T(8,128)}, f32[512]{0:T(512)}) all-reduce(f32[512]{0:T(512)S(1)} %dynamic-slice_convert_fusion.3, ...), channel_id=1, replica_groups=mesh['fsdp'=2,'ctx'=16] {'ctx'}, use_global_device_ids=true, to_apply=%region_20.21 | all-reduce | flops 6295040 | bytes 37777408 | tf_op jit(solution)/shard_map/psum | solution.py:395
  (259 shorter events, 292.1 us)
Async XLA Ops:
  7.2 84.0 %all-gather.10.cloned.1.call-start = ((), (), s32[]{:S(2)}) async-start(), calls=%async_computation.5 | async-start | bytes 9437184 | tf_op jit(solution)/shard_map/all_gather | solution.py:123
  8.0 117.9 %all-gather.16.cloned.1.call-start = ((), (), s32[]{:S(2)}) async-start(), calls=%async_computation.8 | async-start | bytes 3145728 | tf_op jit(solution)/shard_map/all_gather | solution.py:124
  8.7 196.6 %all-gather.12.cloned.1.call-start = ((), (), s32[]{:S(2)}) async-start(), calls=%async_computation.6 | async-start | bytes 8912896 | tf_op jit(solution)/shard_map/all_gather | solution.py:165
  8.8 98.9 %copy-start.28 = (pred[128]{0:T(512)(128)(4,1)}, pred[128]{0:T(512)(128)(4,1)S(1)}, u32[]{:S(2)}) copy-start(pred[128]{0:T(512)(128)(4,1)S(1)} %get-tuple-element.817) | copy-start | bytes 388
  8.8 98.8 %copy-start.35 = (pred[128]{0:T(512)(128)(4,1)}, pred[128]{0:T(512)(128)(4,1)S(1)}, u32[]{:S(2)}) copy-start(pred[128]{0:T(512)(128)(4,1)S(1)} %get-tuple-element.816) | copy-start | bytes 388
  8.8 98.8 %copy-start.37 = (pred[128]{0:T(512)(128)(4,1)}, pred[128]{0:T(512)(128)(4,1)S(1)}, u32[]{:S(2)}) copy-start(pred[128]{0:T(512)(128)(4,1)S(1)} %fusion.168) | copy-start | bytes 388
  15.8 91.8 %copy-start.16 = (f32[128,128]{0,1:T(8,128)}, f32[128,128]{0,1:T(8,128)S(1)}, u32[]{:S(2)}) copy-start(f32[128,128]{0,1:T(8,128)S(1)} %copy.90) | copy-start | bytes 196612
  113.0 171.1 %all-gather.14.cloned.1.call-start = ((), (), s32[]{:S(2)}) async-start(), calls=%async_computation.7 | async-start | bytes 8912896 | tf_op jit(solution)/shard_map/all_gather | solution.py:166
  115.9 428.0 %all-gather.20.cloned.1.call-start = ((), (), s32[]{:S(2)}) async-start(), calls=%async_computation.10 | async-start | bytes 12582912 | tf_op jit(solution)/shard_map/all_gather | solution.py:127
  116.5 436.2 %all-gather.18.cloned.1.call-start = ((), (), s32[]{:S(2)}) async-start(), calls=%async_computation.9 | async-start | bytes 12582912 | tf_op jit(solution)/shard_map/all_gather | solution.py:125
  117.1 754.3 %reduce-scatter.6.cloned.1.call-start = ((), (), s32[]{:S(2)}) async-start(), calls=%async_computation.11 | async-start | bytes 35651584 | tf_op jit(solution)/shard_map/reduce_scatter | solution.py:326
  539.8 433.6 %reduce-scatter.12.cloned.1.call-start = ((), (), s32[]{:S(2)}) async-start(), calls=%async_computation.14 | async-start | bytes 12582912 | tf_op jit(solution)/shard_map/reduce_scatter | solution.py:379
  574.3 500.7 %reduce-scatter.14.cloned.1.call-start = ((), (), s32[]{:S(2)}) async-start(), calls=%async_computation.15 | async-start | bytes 12582912 | tf_op jit(solution)/shard_map/reduce_scatter | solution.py:385
  584.9 524.7 %reduce-scatter.10.cloned.1.call-start = ((), (), s32[]{:S(2)}) async-start(), calls=%async_computation.13 | async-start | bytes 3145728 | tf_op jit(solution)/shard_map/reduce_scatter | solution.py:376
  592.8 597.2 %reduce-scatter.8.cloned.1.call-start = ((), (), s32[]{:S(2)}) async-start(), calls=%async_computation.12 | async-start | bytes 9437184 | tf_op jit(solution)/shard_map/reduce_scatter | solution.py:373
  643.5 230.5 %copy-start.17 = (f32[128,128]{0,1:T(8,128)S(1)}, f32[128,128]{0,1:T(8,128)}, u32[]{:S(2)}) copy-start(f32[128,128]{0,1:T(8,128)} %copy-done.16) | copy-start | bytes 196612
  643.5 230.5 %copy-start.19 = (f32[128,128]{0,1:T(8,128)S(1)}, f32[128,128]{0,1:T(8,128)}, u32[]{:S(2)}) copy-start(f32[128,128]{0,1:T(8,128)} %copy-done.18) | copy-start | bytes 196612
  643.5 230.5 %copy-start.29 = (pred[128]{0:T(512)(128)(4,1)S(1)}, pred[128]{0:T(512)(128)(4,1)}, u32[]{:S(2)}) copy-start(pred[128]{0:T(512)(128)(4,1)} %copy-done.28) | copy-start | bytes 388
  643.5 230.5 %copy-start.31 = (s32[128]{0:T(128)S(1)}, s32[128]{0:T(128)}, u32[]{:S(2)}) copy-start(s32[128]{0:T(128)} %copy-done.30) | copy-start | bytes 1540
  643.5 230.5 %copy-start.36 = (pred[128]{0:T(512)(128)(4,1)S(1)}, pred[128]{0:T(512)(128)(4,1)}, u32[]{:S(2)}) copy-start(pred[128]{0:T(512)(128)(4,1)} %copy-done.35) | copy-start | bytes 388
  643.5 230.5 %copy-start.38 = (pred[128]{0:T(512)(128)(4,1)S(1)}, pred[128]{0:T(512)(128)(4,1)}, u32[]{:S(2)}) copy-start(pred[128]{0:T(512)(128)(4,1)} %copy-done.37) | copy-start | bytes 388
  643.5 230.5 %copy-start.40 = (s32[128]{0:T(128)S(1)}, s32[128]{0:T(128)}, u32[]{:S(2)}) copy-start(s32[128]{0:T(128)} %copy-done.39) | copy-start | bytes 1540
  643.5 230.5 %copy-start.42 = (s32[128]{0:T(128)S(1)}, s32[128]{0:T(128)}, u32[]{:S(2)}) copy-start(s32[128]{0:T(128)} %copy-done.41) | copy-start | bytes 1540
  913.4 201.6 %copy-start.26 = (f32[256]{0:T(256)S(1)}, f32[256]{0:T(256)}, u32[]{:S(2)}) copy-start(f32[256]{0:T(256)} %copy-done.25) | copy-start | bytes 3076
  (39 other events, 931.6 us)
Sparse Core Ops, SparseCore 0:
  9.6 81.5 all-gather.9
  92.7 33.0 all-gather.15
  128.6 76.6 all-gather.11
  207.9 76.2 all-gather.13
  285.6 103.5 all-gather.19
  390.6 103.9 all-gather.17
  539.9 331.4 reduce-scatter.5
  873.6 99.6 reduce-scatter.11
  975.7 99.2 reduce-scatter.13
  1077.7 31.8 reduce-scatter.9
  1112.5 77.3 reduce-scatter.7
where the time goes:
time: 1730 us
  waiting for transfers between devices  723 us (42%)
  blocking collectives  549 us (32%)
  matrix products  257 us (15%)
  local copies, waits for them, and re-layouts  115 us (7%)
  other arithmetic  52.1 us (3%)
    psum x1, blocking collectives, per_device(): lax.psum((share_gain, share_shift, share_qkv, share_out, share_up, share_...  531 us
    reduce_scatter x1, waiting for transfers between devices, per_device(): lax.psum_scatter(blocks_out.reshape(seq_rows * lax.axis_size('ctx'), seq_...  228 us
    reduce_scatter x1, waiting for transfers between devices, per_device(): lax.psum_scatter(down_wgrad.astype(jnp.bfloat16), 'fsdp', scatter_dimensi...  102 us
    all_gather x1, waiting for transfers between devices, per_device(): piece_keys = lax.all_gather(key_rows, 'ctx', axis=0, tiled=True)  75.3 us
    all_gather x1, waiting for transfers between devices, per_device(): lax.all_gather(qkv_weight, 'fsdp', axis=1, tiled=True)  74.7 us
    all_gather x1, waiting for transfers between devices, per_device(): piece_values = lax.all_gather(value_rows, 'ctx', axis=0, tiled=True)  70.7 us
    reduce_scatter x1, waiting for transfers between devices, per_device(): lax.psum_scatter(qkv_wgrad.astype(jnp.bfloat16), 'fsdp', scatter_dimensio...  67.6 us
    reduce_scatter x1, waiting for transfers between devices, per_device(): lax.psum_scatter(up_wgrad.astype(jnp.bfloat16), 'fsdp', scatter_dimension...  59.9 us
  transfers between devices with their start and end apart: 11, of which 9 were waited for; matrix products, arithmetic and copies ran while one was open for 24% of the time, Pallas kernels for 0%

commit v1 on v0

--- a/solution.py
+++ b/solution.py
@@ -1,8 +1,11 @@
+import functools
 import math
 
 import jax
 import jax.numpy as jnp
 from jax import lax
+from jax.experimental import pallas as pl
+from jax.experimental.pallas import tpu as pltpu
 from jax.sharding import PartitionSpec as P
 
 D = 1024
@@ -420,6 +423,1001 @@
     )
 
 
+F32 = jnp.float32
+BF16 = jnp.bfloat16
+FF = 4096
+FSDP = 2
+CHIPS = 8
+ROWS = SEQ_DEV_TOK * SEQS
+ALL = 4 * ROWS
+LENGTH = CHIPS * 2 * SEQ_DEV_TOK
+HALF = SEQ_DEV_TOK // 2
+QB = 256
+NCH = 12
+MASKS = (1, 2, 4)
+SCALE = HEAD_DIM**-0.5
+
+
+def fits(mesh):
+    return mesh.shape["fsdp"] == FSDP and mesh.shape["ctx"] == 2 * CHIPS
+
+
+def dot(left, right):
+    return lax.dot_general(left, right, (((1,), (0,)), ((), ())), preferred_element_type=F32)
+
+
+def dot_nt(left, right):
+    return lax.dot_general(left, right, (((1,), (1,)), ((), ())), preferred_element_type=F32)
+
+
+def dot_tn(left, right):
+    return lax.dot_general(left, right, (((0,), (0,)), ((), ())), preferred_element_type=F32)
+
+
+def turn(values, cosine, sine):
+    lane = lax.broadcasted_iota(jnp.int32, values.shape, 1)
+    width = values.shape[1]
+    other = jnp.where(
+        lane % 2 == 0, pltpu.roll(values, width - 1, 1), pltpu.roll(values, 1, 1)
+    )
+    return values * cosine + other * sine
+
+
+def gate(values):
+    inner = 0.7978845608028654 * (values + 0.044715 * values * values * values)
+    th = jnp.tanh(inner)
+    half = 0.5 * (1.0 + th)
+    slope = half + (0.5 * values) * (1.0 - th * th) * (
+        0.7978845608028654 * (1.0 + 3 * 0.044715 * values * values)
+    )
+    return values * half, slope
+
+
+def fused_kernel(
+    places_ref,
+    halves_ref,
+    blocks_ref,
+    vec_ref,
+    upb_ref,
+    cos_ref,
+    sin_ref,
+    scos_ref,
+    ssin_ref,
+    tok_ref,
+    cot_ref,
+    wqkv_h,
+    wout_h,
+    wup_h,
+    wdn_h,
+    mixed_ref,
+    tgrad_ref,
+    small_ref,
+    odn,
+    oup,
+    oqkv,
+    oout,
+    vall,
+    xs,
+    nrm,
+    gal,
+    wq,
+    wout,
+    wup,
+    wdn,
+    hid,
+    upg,
+    sbuf,
+    rbuf,
+    aq,
+    ag,
+    ak,
+    av,
+    akt,
+    avt,
+    agt,
+    sco,
+    dka,
+    dva,
+    osrt,
+    rb2,
+    aall,
+    dqkv,
+    mats,
+    rs0,
+    rs1,
+    rs2,
+    xsw,
+    own_acc,
+    red_s,
+    red_x,
+    red_r,
+    red_xr,
+    sm,
+    smg,
+    sma,
+    lsem,
+    gsend,
+    grecv,
+    asend,
+    arecv,
+    osend,
+    orecv,
+    rssend,
+    rsrecv,
+    agsend,
+    agrecv,
+    clocal,
+    csend,
+    crecv,
+    dsend,
+    drecv,
+    smsend,
+    smrecv,
+):
+    f = lax.axis_index("fsdp")
+    c = lax.axis_index("ctx")
+    k = c % 2
+    p = c // 2
+    zz = p // 2
+    yy = p % 2
+    xpart = (1 - f, c)
+    sibling = (f, 2 * p + 1 - k)
+    diagonal = (1 - f, 2 * p + 1 - k)
+    own = 2 * f + k
+    sibb = 2 * f + 1 - k
+    xb = 2 * (1 - f) + k
+    dg = 2 * (1 - f) + 1 - k
+    MESH = pl.DeviceIdType.MESH
+
+    def member(q):
+        return (f, 2 * q + k)
+
+    def remote(src, dst, ssem, rsem, device):
+        return pltpu.make_async_remote_copy(
+            src_ref=src,
+            dst_ref=dst,
+            send_sem=ssem,
+            recv_sem=rsem,
+            device_id=device,
+            device_id_type=MESH,
+        )
+
+    def rows(b):
+        return pl.ds(pl.multiple_of(b * ROWS, ROWS), ROWS)
+
+    def lanes(i, n):
+        return pl.ds(pl.multiple_of(i * n, n), n)
+
+    loads = [
+        pltpu.make_async_copy(wqkv_h.at[:, lanes(k, 256)], wq.at[f], lsem.at[0]),
+        pltpu.make_async_copy(
+            wqkv_h.at[:, pl.ds(pl.multiple_of(1024 + 256 * k, 256), 256)], wq.at[1 + f], lsem.at[1]
+        ),
+        pltpu.make_async_copy(wup_h.at[:, lanes(k, 1024)], wup, lsem.at[2]),
+        pltpu.make_async_copy(wdn_h.at[lanes(k, 1024), :], wdn, lsem.at[3]),
+        pltpu.make_async_copy(wout_h.at[lanes(k, 256), :], wout, lsem.at[4]),
+    ]
+    for load in loads:
+        load.start()
+
+    barrier = pltpu.get_barrier_semaphore()
+    for device in [xpart, sibling, diagonal] + [member(p ^ i) for i in range(1, CHIPS)]:
+        pl.semaphore_signal(barrier, inc=1, device_id=device, device_id_type=MESH)
+    pl.semaphore_wait(barrier, 3 + CHIPS - 1)
+
+    vec_copy = remote(vec_ref, vall.at[f], gsend.at[0], grecv.at[0], xpart)
+    vec_copy.start()
+    swap_copy = remote(
+        wqkv_h.at[:, pl.ds(pl.multiple_of(512 + 256 * k, 256), 256)],
+        wq.at[2 * f],
+        gsend.at[1],
+        grecv.at[1],
+        xpart,
+    )
+    swap_copy.start()
+    vall[f] = vec_ref[...]
+    vec_copy.wait()
+    gain = jnp.concatenate([vall[0, 0:1, :], vall[1, 0:1, :]], axis=1).astype(F32)
+    shift = jnp.concatenate([vall[0, 1:2, :], vall[1, 1:2, :]], axis=1).astype(F32)
+    down_b = jnp.concatenate([vall[0, 2:3, :], vall[1, 2:3, :]], axis=1).astype(F32)
+
+    step = 64
+
+    def norm_rows(i, carry):
+        here = pl.ds(pl.multiple_of(i * step, step), step)
+        there = pl.ds(pl.multiple_of(own * ROWS + i * step, step), step)
+        row = lax.broadcasted_iota(jnp.int32, (step, ROWS), 0) + i * step
+        col = lax.broadcasted_iota(jnp.int32, (step, ROWS), 1)
+        pick = (col == 2 * (row % SEQ_DEV_TOK) + row // SEQ_DEV_TOK).astype(F32).astype(BF16)
+        values = dot(pick, tok_ref[...])
+        gal[there, :] = dot(pick, cot_ref[...]).astype(BF16)
+        xs[here, :] = values.astype(BF16)
+        center = values - jnp.mean(values, axis=1, keepdims=True)
+        spread = jnp.mean(center * center, axis=1, keepdims=True)
+        nrm[there, :] = (center * lax.rsqrt(spread + EPS) * gain + shift).astype(BF16)
+        return carry
+
+    lax.fori_loop(0, ROWS // step, norm_rows, 0)
+
+    def spread_copy(buf, b, n, device):
+        return remote(buf.at[rows(b)], buf.at[rows(b)], gsend.at[n], grecv.at[n], device)
+
+    n_sib = spread_copy(nrm, own, 2, sibling)
+    n_x = spread_copy(nrm, own, 3, xpart)
+    g_sib = spread_copy(gal, own, 4, sibling)
+    g_x = spread_copy(gal, own, 5, xpart)
+    for copy in (n_sib, n_x, g_sib, g_x):
+        copy.start()
+    for load in loads:
+        load.wait()
+
+    def feed_block(b):
+        def part(i, carry):
+            cols = lanes(i, 256)
+            up = dot(nrm[rows(b), :], wup[:, cols]) + upb_ref[0:1, cols].astype(F32)
+            value, slope = gate(up)
+            hid[rows(b), cols] = value.astype(BF16)
+            back = dot_nt(gal[rows(b), :], wdn[cols, :])
+            upg[rows(b), cols] = (back * slope).astype(BF16)
+            return carry
+
+        lax.fori_loop(0, 4, part, 0)
+
+    def put_heads(first, second, fq, kq, t):
+        for h in range(4):
+            sbuf[2 * h + fq, t, kq] = jnp.concatenate(
+                [first[:, 64 * h : 64 * h + 64], second[:, 64 * h : 64 * h + 64]], axis=1
+            ).reshape(4, HALF, 128)
+
+    def turned(values, kq):
+        parts = []
+        for s in range(SEQS):
+            line = []
+            for half in range(2):
+                piece = values[128 * s : 128 * s + 128, 128 * half : 128 * half + 128]
+                line.append(turn(piece, cos_ref[kq], sin_ref[kq]))
+            parts.append(jnp.concatenate(line, axis=1))
+        return jnp.concatenate(parts, axis=0).astype(BF16)
+
+    def qk_block(b, fq, kq):
+        normed = nrm[rows(b), :]
+        query = dot(normed, wq[0])
+        key = dot(normed, wq[1])
+        put_heads(turned(query, kq) * BF16(SCALE), turned(key, kq), fq, kq, 0)
+
+    def vg_block(b, fq, kq):
+        value = dot(nrm[rows(b), :], wq[2]).astype(BF16)
+        grads = dot_nt(gal[rows(b), :], wout[...]).astype(BF16)
+        put_heads(value, grads, fq, kq, 1)
+
+    def in_copy(q, t, kq):
+        return remote(
+            sbuf.at[q, t, kq],
+            rbuf.at[2 * p + kq, t],
+            asend.at[q, t, kq],
+            arecv.at[p, t, kq],
+            member(q),
+        )
+
+    def send_block(fq, kq, t):
+        for i in range(4):
+            q = 2 * (zz ^ i) + fq
+            if i == 0:
+
+                @pl.when(fq == yy)
+                def _():
+                    pltpu.make_async_copy(
+                        sbuf.at[q, t, kq], rbuf.at[2 * p + kq, t], arecv.at[p, t, kq]
+                    ).start()
+
+                @pl.when(fq != yy)
+                def _():
+                    in_copy(q, t, kq).start()
+            else:
+                in_copy(q, t, kq).start()
+
+    def sent_block(fq, kq, t):
+        for i in range(4):
+            q = 2 * (zz ^ i) + fq
+            if i == 0:
+
+                @pl.when(fq != yy)
+                def _():
+                    in_copy(q, t, kq).wait_send()
+            else:
+                in_copy(q, t, kq).wait_send()
+
+    feed_block(own)
+    n_sib.wait_recv()
+    g_sib.wait_recv()
+    feed_block(sibb)
+    swap_copy.wait_recv()
+    for b, kq in ((own, k), (sibb, 1 - k)):
+        qk_block(b, f, kq)
+        send_block(f, kq, 0)
+        vg_block(b, f, kq)
+        send_block(f, kq, 1)
+    n_x.wait_recv()
+    n_dg = spread_copy(nrm, xb, 6, sibling)
+    n_dg.start()
+    qk_block(xb, 1 - f, k)
+    send_block(1 - f, k, 0)
+    n_dg.wait_recv()
+    qk_block(dg, 1 - f, 1 - k)
+    send_block(1 - f, 1 - k, 0)
+    g_x.wait_recv()
+    g_dg = spread_copy(gal, xb, 7, sibling)
+    g_dg.start()
+    vg_block(xb, 1 - f, k)
+    send_block(1 - f, k, 1)
+    g_dg.wait_recv()
+    vg_block(dg, 1 - f, 1 - k)
+    send_block(1 - f, 1 - k, 1)
+    feed_block(xb)
+    feed_block(dg)
+
+    def down_part(i, carry):
+        full = dot_tn(hid[:, lanes(i, 256)], gal[...]).astype(BF16)
+        for cc in range(4):
+            mats[cc, lanes(i, 256), :] = full[:, 256 * cc : 256 * cc + 256]
+        return carry
+
+    lax.fori_loop(0, 4, down_part, 0)
+
+    def up_part(i, carry):
+        full = dot_tn(nrm[:, lanes(i, 256)], upg[...]).astype(BF16)
+        for cc in range(4):
+            mats[4 + cc, lanes(i, 256), :] = full[:, 256 * cc : 256 * cc + 256]
+        return carry
+
+    lax.fori_loop(0, 4, up_part, 0)
+
+    sm[...] = jnp.zeros_like(sm)
+    sm[0:1, :] = jnp.sum(upg[...].astype(F32), axis=0, keepdims=True)
+    sm[2:3, :] = jnp.sum(gal[...].astype(F32), axis=0, keepdims=True)
+
+    def bit(mask):
+        return (p // mask) % 2
+
+    def base(ph):
+        at = 0
+        for j in range(ph):
+            at = at + bit(MASKS[j]) * (512 >> j)
+        return at
+
+    rsb = (rs0, rs1, rs2)
+
+    def chunk_rows(ph, side, n):
+        return pl.ds(pl.multiple_of(base(ph) + side * n, n), n)
+
+    def rs_copy(ch, ph):
+        n = 512 >> ph
+        side = bit(MASKS[ph])
+        return remote(
+            mats.at[ch, chunk_rows(ph, 1 - side, n)],
+            rsb[ph].at[ch],
+            rssend.at[ch, ph],
+            rsrecv.at[ch, ph],
+            member(p ^ MASKS[ph]),
+        )
+
+    def rs_add(ch, ph):
+        n = 512 >> ph
+        at = base(ph) + bit(MASKS[ph]) * n
+        rs_copy(ch, ph).wait_recv()
+
+        def add(i, carry):
+            here = pl.ds(pl.multiple_of(at + i * 128, 128), 128)
+            there = pl.ds(pl.multiple_of(i * 128, 128), 128)
+            mats[ch, here, :] = (
+                mats[ch, here, :].astype(F32) + rsb[ph][ch, there, :].astype(F32)
+            ).astype(BF16)
+            return carry
+
+        lax.fori_loop(0, n // 128, add, 0)
+
+    def out_slice(ch, kk, at, n):
+        there = pl.ds(pl.multiple_of(at, n), n)
+        if ch < 4:
+            return odn.at[pl.ds(pl.multiple_of(kk * 1024 + at, n), n), 256 * ch : 256 * ch + 256]
+        if ch < 8:
+            cols = pl.ds(pl.multiple_of(kk * 1024 + (ch - 4) * 256, 256), 256)
+            return oup.at[there, cols]
+        if ch < 11:
+            start = (0, 1024, 512)[ch - 8]
+            return oqkv.at[there, pl.ds(pl.multiple_of(start + kk * 256, 256), 256)]
+        return oout.at[there, pl.ds(pl.multiple_of(kk * 256, 256), 256)]
+
+    def shard(ch):
+        if ch == 10:
+            return xsw
+        return mats.at[ch, pl.ds(pl.multiple_of(base(3), 128), 128)]
+
+    def swap_shard():
+        return remote(
+            mats.at[10, pl.ds(pl.multiple_of(base(3), 128), 128)],
+            xsw,
+            gsend.at[8],
+            grecv.at[8],
+            xpart,
+        )
+
+    def local_copy(ch):
+        return pltpu.make_async_copy(shard(ch), out_slice(ch, k, base(3), 128), clocal.at[ch])
+
+    def ag_copy(ch, ph):
+        n = 512 >> ph
+        at = base(ph) + bit(MASKS[ph]) * n
+        src = shard(ch) if ph == 2 else out_slice(ch, k, at, n)
+        return remote(
+            src,
+            out_slice(ch, k, at, n),
+            agsend.at[ch, ph],
+            agrecv.at[ch, ph],
+            member(p ^ MASKS[ph]),
+        )
+
+    def core_copy(ch):
+        return remote(
+            out_slice(ch, k, 0, 1024),
+            out_slice(ch, k, 0, 1024),
+            csend.at[ch],
+            crecv.at[ch],
+            sibling,
+        )
+
+    def advance(ch, stage):
+        if stage == 0:
+            rs_copy(ch, 0).start()
+        elif stage <= 2:
+            rs_add(ch, stage - 1)
+            rs_copy(ch, stage).start()
+        elif stage == 3:
+            rs_add(ch, 2)
+            if ch == 10:
+                swap_shard().start()
+                swap_shard().wait_recv()
+            local_copy(ch).start()
+            ag_copy(ch, 2).start()
+        elif stage == 4:
+            ag_copy(ch, 2).wait_recv()
+            local_copy(ch).wait()
+            ag_copy(ch, 1).start()
+        elif stage == 5:
+            ag_copy(ch, 1).wait_recv()
+            ag_copy(ch, 0).start()
+        elif stage == 6:
+            ag_copy(ch, 0).wait_recv()
+            core_copy(ch).start()
+        elif stage == 7:
+            core_copy(ch).wait_recv()
+
+    def settle(ch):
+        for ph in range(3):
+            rs_copy(ch, ph).wait_send()
+            ag_copy(ch, ph).wait_send()
+        core_copy(ch).wait_send()
+        if ch == 10:
+            swap_shard().wait_send()
+
+    for ch in range(8):
+        advance(ch, 0)
+
+    for fq, kq in ((f, k), (f, 1 - k), (1 - f, k), (1 - f, 1 - k)):
+        for t in range(2):
+            sent_block(fq, kq, t)
+    for q in range(CHIPS):
+        for t in range(2):
+            for kq in range(2):
+                pltpu.make_async_copy(
+                    rbuf.at[2 * q + kq, t], rbuf.at[2 * q + kq, t], arecv.at[q, t, kq]
+                ).wait()
+
+    def load_half(place, t, u):
+        return rbuf[places_ref[place], t, 2 * u + halves_ref[place]]
+
+    def sort_rows(i, carry):
+        for u in range(SEQS):
+            here = pl.ds(pl.multiple_of(i * 128, 128), 128)
+            qk = jnp.concatenate([load_half(2 * i, 0, u), load_half(2 * i + 1, 0, u)], axis=0)
+            vg = jnp.concatenate([load_half(2 * i, 1, u), load_half(2 * i + 1, 1, u)], axis=0)
+            aq[u, here, :] = qk[:, :64]
+            ak[u, here, :] = qk[:, 64:]
+            av[u, here, :] = vg[:, :64]
+            ag[u, here, :] = vg[:, 64:]
+            akt[u, :, here] = qk.T[64:, :]
+            vgt = vg.T
+            avt[u, :, here] = vgt[:64, :]
+            agt[u, :, here] = vgt[64:, :]
+        return carry
+
+    lax.fori_loop(0, LENGTH // 128, sort_rows, 0)
+
+    def spot(i):
+        return pl.ds(pl.multiple_of(i * QB, QB), QB)
+
+    def query_block(u, qb):
+        query = aq[u, spot(qb), :]
+        grads = ag[u, spot(qb), :]
+
+        def fold(values):
+            return values.reshape(QB // 8, 8, QB)
+
+        def scores(kb, top):
+            tile = dot_nt(ak[u, spot(kb), :], query)
+            sco[spot(kb), :] = tile
+            return jnp.maximum(top, jnp.max(fold(tile), axis=0))
+
+        top = lax.fori_loop(0, qb, scores, jnp.full((8, QB), masked_score, F32))
+        tile = dot_nt(ak[u, spot(qb), :], query)
+        row = lax.broadcasted_iota(jnp.int32, (QB, QB), 0)
+        col = lax.broadcasted_iota(jnp.int32, (QB, QB), 1)
+        tile = jnp.where(row <= col, tile, masked_score)
+        sco[spot(qb), :] = tile
+        top = jnp.maximum(top, jnp.max(fold(tile), axis=0))
+        top = jnp.max(top, axis=0, keepdims=True)
+
+        def weigh(kb, carry):
+            total, mix = carry
+            weights = jnp.exp(sco[spot(kb), :] - top)
+            sco[spot(kb), :] = weights
+            total = total + jnp.sum(fold(weights), axis=0)
+            mix = mix + dot(avt[u, :, spot(kb)], weights.astype(BF16))
+            return total, mix
+
+        total, mix = lax.fori_loop(
+            0, qb + 1, weigh, (jnp.zeros((8, QB), F32), jnp.zeros((HEAD_DIM, QB), F32))
+        )
+        inverse = 1.0 / jnp.sum(total, axis=0, keepdims=True)
+        mix = mix * inverse
+        dots = jnp.sum(agt[u, :, spot(qb)].astype(F32) * mix, axis=0, keepdims=True)
+
+        def backward(kb, back):
+            chances = sco[spot(kb), :] * inverse
+            slopes = dot_nt(av[u, spot(kb), :], grads)
+            score_grads = (chances * (slopes - dots)).astype(BF16)
+            dva[spot(kb), :] += dot(chances.astype(BF16), grads)
+            dka[spot(kb), :] += dot(score_grads, query)
+            return back + dot(akt[u, :, spot(kb)], score_grads)
+
+        back = lax.fori_loop(0, qb + 1, backward, jnp.zeros((HEAD_DIM, QB), F32))
+        both = jnp.concatenate([mix, back * SCALE], axis=0).T
+        both = turn(both, scos_ref[spot(qb), :], ssin_ref[spot(qb), :]).astype(BF16)
+        osrt[0, pl.ds(qb * (QB // HALF), QB // HALF)] = both.reshape(QB // HALF, HALF, 128)
+
+    def unit(u):
+        dka[...] = jnp.zeros_like(dka)
+        dva[...] = jnp.zeros_like(dva)
+
+        def one(qb, carry):
+            query_block(u, qb)
+            return carry
+
+        lax.fori_loop(0, LENGTH // QB, one, 0)
+
+        def pack(i, carry):
+            both = jnp.concatenate([dva[spot(i), :], dka[spot(i), :]], axis=1)
+            both = turn(both, scos_ref[spot(i), :], ssin_ref[spot(i), :]).astype(BF16)
+            osrt[1, pl.ds(i * (QB // HALF), QB // HALF)] = both.reshape(QB // HALF, HALF, 128)
+            return carry
+
+        lax.fori_loop(0, LENGTH // QB, pack, 0)
+
+        def unsort(i, carry):
+            for t in range(2):
+                for half in range(2):
+                    sbuf[i // 2, u, t, 2 * (i % 2) + half] = osrt[t, blocks_ref[2 * i + half]]
+            return carry
+
+        lax.fori_loop(0, 2 * CHIPS, unsort, 0)
+        for i in range(CHIPS):
+            q = p ^ i
+            if i == 0:
+                pltpu.make_async_copy(sbuf.at[p, u], rb2.at[p, u], orecv.at[p, u]).start()
+            else:
+                out_copy(q, u).start()
+
+    def out_copy(q, u):
+        return remote(
+            sbuf.at[q, u], rb2.at[p, u], osend.at[q, u], orecv.at[p, u], member(q)
+        )
+
+    unit(0)
+    for ch in range(4):
+        advance(ch, 1)
+    unit(1)
+    for ch in range(4, 8):
+        advance(ch, 1)
+    for ch in range(4):
+        advance(ch, 2)
+
+    for q in range(CHIPS):
+        for u in range(SEQS):
+            pltpu.make_async_copy(rb2.at[q, u], rb2.at[q, u], orecv.at[q, u]).wait()
+
+    for fq in range(2):
+        for kq in range(2):
+            for u in range(SEQS):
+                at = (2 * fq + kq) * ROWS + u * 128
+                here = slice(at, at + 128)
+                two = slice(2 * kq, 2 * kq + 2)
+                for pair in range(2):
+                    cols = slice(128 * pair, 128 * pair + 128)
+                    x0 = rb2[4 * pair + fq, u, 0, two].reshape(128, 128)
+                    x1 = rb2[4 * pair + 2 + fq, u, 0, two].reshape(128, 128)
+                    y0 = rb2[4 * pair + fq, u, 1, two].reshape(128, 128)
+                    y1 = rb2[4 * pair + 2 + fq, u, 1, two].reshape(128, 128)
+                    aall[here, cols] = jnp.concatenate([x0[:, :64], x1[:, :64]], axis=1)
+                    dqkv[0, here, cols] = jnp.concatenate([x0[:, 64:], x1[:, 64:]], axis=1)
+                    dqkv[2, here, cols] = jnp.concatenate([y0[:, :64], y1[:, :64]], axis=1)
+                    dqkv[1, here, cols] = jnp.concatenate([y0[:, 64:], y1[:, 64:]], axis=1)
+
+    def att_part(i, carry):
+        here = lanes(i, 256)
+        left = nrm[:, here]
+        for slot in range(3):
+            at = 8 + (slot - f + 3) % 3
+            mats[at, here, :] = dot_tn(left, dqkv[slot]).astype(BF16)
+        mats[11, here, :] = dot_tn(gal[:, here], aall[...]).astype(BF16)
+        return carry
+
+    lax.fori_loop(0, 4, att_part, 0)
+    for ch in range(8, 12):
+        advance(ch, 0)
+
+    def normed_part(b, cols):
+        here = rows(b)
+        total = dot_nt(upg[here, :], wup[cols, :])
+        for slot in range(3):
+            total = total + dot_nt(dqkv[slot, here, :], wq[slot, cols, :])
+        return total
+
+    def mixed_part(b, cols):
+        here = rows(b)
+        return dot(hid[here, :], wdn[:, cols]) + dot(aall[here, :], wout[:, cols])
+
+    def reduce_copies(n):
+        return (
+            remote(red_s.at[n, 0], red_r.at[n, 0], dsend.at[n, 0], drecv.at[n, 0], sibling),
+            remote(red_s.at[n, 1], red_r.at[n, 1], dsend.at[n, 1], drecv.at[n, 1], sibling),
+            remote(red_x.at[n], red_xr.at[n], dsend.at[n, 2], drecv.at[n, 2], xpart),
+        )
+
+    parts = (normed_part, mixed_part)
+
+    def reduce_first(n):
+        copies = reduce_copies(n)
+        for slot, b in ((1, dg), (0, sibb)):
+
+            def fill(i, carry):
+                red_s[n, slot, :, lanes(i, 256)] = parts[n](b, lanes(i, 256)).astype(BF16)
+                return carry
+
+            lax.fori_loop(0, 4, fill, 0)
+            copies[slot].start()
+
+    def reduce_second(n):
+        copies = reduce_copies(n)
+        copies[1].wait_recv()
+
+        def fill(i, carry):
+            cols = lanes(i, 256)
+            red_x[n, :, cols] = (
+                parts[n](xb, cols) + red_r[n, 1, :, cols].astype(F32)
+            ).astype(BF16)
+            return carry
+
+        lax.fori_loop(0, 4, fill, 0)
+        copies[2].start()
+
+    def reduce_third(n):
+        copies = reduce_copies(n)
+
+        def fill(i, carry):
+            cols = lanes(i, 256)
+            own_acc[n, :, cols] = parts[n](own, cols)
+            return carry
+
+        lax.fori_loop(0, 4, fill, 0)
+        copies[0].wait_recv()
+        copies[2].wait_recv()
+
+        def finish(i, carry):
+            cols = lanes(i, 256)
+            own_acc[n, :, cols] = (
+                own_acc[n, :, cols]
+                + red_r[n, 0, :, cols].astype(F32)
+                + red_xr[n, :, cols].astype(F32)
+            )
+            return carry
+
+        lax.fori_loop(0, 4, finish, 0)
+
+    def out_pick():
+        row = lax.broadcasted_iota(jnp.int32, (ROWS, ROWS), 0)
+        col = lax.broadcasted_iota(jnp.int32, (ROWS, ROWS), 1)
+        return (row == 2 * (col % SEQ_DEV_TOK) + col // SEQ_DEV_TOK).astype(F32).astype(BF16)
+
+    reduce_first(0)
+    reduce_second(0)
+    reduce_first(1)
+    reduce_second(1)
+    for ch in range(4, 8):
+        advance(ch, 2)
+    for ch in range(4):
+        advance(ch, 3)
+    reduce_third(0)
+
+    def back_rows(i, carry):
+        dgain, dshift = carry
+        here = pl.ds(pl.multiple_of(i * step, step), step)
+        there = pl.ds(pl.multiple_of(own * ROWS + i * step, step), step)
+        values = xs[here, :].astype(F32)
+        center = values - jnp.mean(values, axis=1, keepdims=True)
+        spread = lax.rsqrt(jnp.mean(center * center, axis=1, keepdims=True) + EPS)
+        hat = center * spread
+        grads = own_acc[0, here, :]
+        dgain = dgain + jnp.sum(grads * hat, axis=0, keepdims=True)
+        dshift = dshift + jnp.sum(grads, axis=0, keepdims=True)
+        inner = grads * gain
+        inner = spread * (
+            inner
+            - jnp.mean(inner, axis=1, keepdims=True)
+            - hat * jnp.mean(inner * hat, axis=1, keepdims=True)
+        )
+        xs2 = gal[there, :].astype(F32) + inner
+        red_s[0, 0, here, :] = xs2.astype(BF16)
+        return dgain, dshift
+
+    reduce_copies(0)[0].wait_send()
+    dgain, dshift = lax.fori_loop(
+        0, ROWS // step, back_rows, (jnp.zeros((1, D), F32), jnp.zeros((1, D), F32))
+    )
+    tgrad_ref[...] = dot(out_pick(), red_s[0, 0]).astype(BF16)
+    sm[3:4, :] = dgain
+    sm[4:5, :] = dshift
+
+    small_copies = [
+        remote(sm, smg.at[own], smsend.at[0], smrecv.at[own], sibling),
+        remote(sm, smg.at[own], smsend.at[1], smrecv.at[own], xpart),
+        remote(sm, smg.at[own], smsend.at[2], smrecv.at[own], diagonal),
+    ]
+    for copy in small_copies:
+        copy.start()
+
+    reduce_third(1)
+    reduce_copies(1)[0].wait_send()
+
+    def mixed_rows(i, carry):
+        here = pl.ds(pl.multiple_of(i * step, step), step)
+        red_s[1, 0, here, :] = (xs[here, :].astype(F32) + own_acc[1, here, :] + down_b).astype(
+            BF16
+        )
+        return carry
+
+    lax.fori_loop(0, ROWS // step, mixed_rows, 0)
+    mixed_ref[...] = dot(out_pick(), red_s[1, 0]).astype(BF16)
+
+    smg[own] = sm[...]
+    for b in (sibb, xb, dg):
+        remote(sm, smg.at[b], smsend.at[0], smrecv.at[b], sibling).wait_recv()
+    for copy in small_copies:
+        copy.wait_send()
+    first_b = 2 * f
+    sma[p, 0:1, :] = smg[first_b, 0:1, :]
+    sma[p, 1:2, :] = smg[first_b + 1, 0:1, :]
+    sma[p, 2:3, :] = sm[2:3, :]
+    sma[p, 3:8, :] = smg[0, 3:8, :] + smg[1, 3:8, :] + smg[2, 3:8, :] + smg[3, 3:8, :]
+    sm_copies = [
+        remote(sma.at[p], sma.at[p], smsend.at[2 + i], smrecv.at[3 + i], member(p ^ i))
+        for i in range(1, CHIPS)
+    ]
+    for copy in sm_copies:
+        copy.start()
+
+    for ch in range(8, 12):
+        advance(ch, 1)
+    for stage in range(4, 8):
+        for ch in range(8):
+            if stage - 1 > 2 or ch >= 4:
+                pass
+            if stage == 4 and ch >= 4:
+                advance(ch, 3)
+            advance(ch, stage)
+        if stage - 2 <= 5:
+            for ch in range(8, 12):
+                advance(ch, stage - 2)
+    for stage in (6, 7):
+        for ch in range(8, 12):
+            advance(ch, stage)
+
+    total = jnp.zeros((8, D), F32)
+    for copy in sm_copies:
+        copy.wait()
+    for q in range(CHIPS):
+        total = total + sma[q]
+    small_ref[...] = total
+
+    for copy in (vec_copy,):
+        pass
+    swap_copy.wait_send()
+    for copy in (n_sib, n_x, g_sib, g_x, n_dg, g_dg):
+        copy.wait_send()
+    for u in range(SEQS):
+        for i in range(1, CHIPS):
+            out_copy(p ^ i, u).wait_send()
+    for n in range(2):
+        copies = reduce_copies(n)
+        copies[1].wait_send()
+        copies[2].wait_send()
+    for ch in range(NCH):
+        settle(ch)
+
+
+def head_tables(places):
+    lane = jnp.arange(HEAD_DIM, dtype=jnp.int32)
+    speeds = 10000.0 ** (-(lane // 2 * 2).astype(F32) / ROT_DIM)
+    phase = places.astype(F32)[:, None] * speeds[None, :]
+    turning = (lane < ROT_DIM)[None, :]
+    sign = jnp.where(lane % 2 == 0, -1.0, 1.0)[None, :]
+    return jnp.where(turning, jnp.cos(phase), 1.0), jnp.where(turning, jnp.sin(phase) * sign, 0.0)
+
+
+def fused_device(
+    tokens,
+    block_pairs,
+    norm_gain,
+    norm_bias,
+    qkv_weight,
+    out_weight,
+    up_weight,
+    up_bias,
+    down_weight,
+    down_bias,
+    cotangent,
+):
+    f = lax.axis_index("fsdp")
+    c = lax.axis_index("ctx")
+    order = jnp.stack((block_pairs, 4 * CHIPS - 1 - block_pairs), axis=1).reshape(4 * CHIPS)
+    hits = order[None, :] == jnp.arange(4 * CHIPS, dtype=jnp.int32)[:, None]
+    places = jnp.sum(
+        jnp.where(hits, jnp.arange(4 * CHIPS, dtype=jnp.int32)[None, :], 0), axis=1
+    ).astype(jnp.int32)
+    holders = places // 2
+    halves = places % 2
+    first = lax.dynamic_slice(block_pairs, (c // 2 * 2,), (2,))
+    row = jnp.arange(SEQ_DEV_TOK, dtype=jnp.int32)
+    blocks = jnp.where(row[None, :] < HALF, first[:, None], 4 * CHIPS - 1 - first[:, None])
+    own_places = (blocks * HALF + row[None, :] % HALF).reshape(-1)
+    cosine, sine = head_tables(own_places)
+    cos_tab = jnp.tile(cosine, (1, 2)).reshape(2, SEQ_DEV_TOK, 128)
+    sin_tab = jnp.tile(sine, (1, 2)).reshape(2, SEQ_DEV_TOK, 128)
+    all_cos, all_sin = head_tables(jnp.arange(LENGTH, dtype=jnp.int32))
+    scos = jnp.concatenate((jnp.ones_like(all_cos), all_cos), axis=1)
+    ssin = jnp.concatenate((jnp.zeros_like(all_sin), -all_sin), axis=1)
+    vec = jnp.concatenate(
+        (
+            norm_gain[None],
+            norm_bias[None],
+            down_bias[None],
+            jnp.zeros((13, norm_gain.shape[0]), BF16),
+        ),
+        axis=0,
+    )
+    upb = lax.dynamic_slice(up_bias, (c % 2 * 1024,), (1024,))[None]
+
+    vm = pl.BlockSpec(memory_space=pltpu.VMEM)
+    sme = pl.BlockSpec(memory_space=pltpu.SMEM)
+    hbm = pl.BlockSpec(memory_space=pl.ANY)
+    dma = pltpu.SemaphoreType.DMA
+    scratch = [
+        pltpu.VMEM((2, 16, 512), BF16),
+        pltpu.VMEM((ROWS, D), BF16),
+        pltpu.VMEM((ALL, D), BF16),
+        pltpu.VMEM((ALL, D), BF16),
+        pltpu.VMEM((3, D, 256), BF16),
+        pltpu.VMEM((256, D), BF16),
+        pltpu.VMEM((D, 1024), BF16),
+        pltpu.VMEM((1024, D), BF16),
+        pltpu.VMEM((ALL, 1024), BF16),
+        pltpu.VMEM((ALL, 1024), BF16),
+        pltpu.VMEM((CHIPS, 2, 2, 4, HALF, 128), BF16),
+        pltpu.VMEM((2 * CHIPS, 2, 4, HALF, 128), BF16),
+        pltpu.VMEM((SEQS, LENGTH, HEAD_DIM), BF16),
+        pltpu.VMEM((SEQS, LENGTH, HEAD_DIM), BF16),
+        pltpu.VMEM((SEQS, LENGTH, HEAD_DIM), BF16),
+        pltpu.VMEM((SEQS, LENGTH, HEAD_DIM), BF16),
+        pltpu.VMEM((SEQS, HEAD_DIM, LENGTH), BF16),
+        pltpu.VMEM((SEQS, HEAD_DIM, LENGTH), BF16),
+        pltpu.VMEM((SEQS, HEAD_DIM, LENGTH), BF16),
+        pltpu.VMEM((LENGTH, QB), F32),
+        pltpu.VMEM((LENGTH, HEAD_DIM), F32),
+        pltpu.VMEM((LENGTH, HEAD_DIM), F32),
+        pltpu.VMEM((2, 4 * CHIPS, HALF, 128), BF16),
+        pltpu.VMEM((CHIPS, SEQS, 2, 4, HALF, 128), BF16),
+        pltpu.VMEM((ALL, 256), BF16),
+        pltpu.VMEM((3, ALL, 256), BF16),
+        pltpu.VMEM((NCH, 1024, 256), BF16),
+        pltpu.VMEM((NCH, 512, 256), BF16),
+        pltpu.VMEM((NCH, 256, 256), BF16),
+        pltpu.VMEM((NCH, 128, 256), BF16),
+        pltpu.VMEM((128, 256), BF16),
+        pltpu.VMEM((2, ROWS, D), F32),
+        pltpu.VMEM((2, 2, ROWS, D), BF16),
+        pltpu.VMEM((2, ROWS, D), BF16),
+        pltpu.VMEM((2, 2, ROWS, D), BF16),
+        pltpu.VMEM((2, ROWS, D), BF16),
+        pltpu.VMEM((8, D), F32),
+        pltpu.VMEM((4, 8, D), F32),
+        pltpu.VMEM((CHIPS, 8, D), F32),
+        dma((5,)),
+        dma((9,)),
+        dma((9,)),
+        dma((CHIPS, 2, 2)),
+        dma((CHIPS, 2, 2)),
+        dma((CHIPS, SEQS)),
+        dma((CHIPS, SEQS)),
+        dma((NCH, 3)),
+        dma((NCH, 3)),
+        dma((NCH, 3)),
+        dma((NCH, 3)),
+        dma((NCH,)),
+        dma((NCH,)),
+        dma((NCH,)),
+        dma((2, 3)),
+        dma((2, 3)),
+        dma((10,)),
+        dma((11,)),
+    ]
+    mixed, tokens_grad, small, dn, up, qkv, out_t = pl.pallas_call(
+        fused_kernel,
+        out_shape=(
+            jax.ShapeDtypeStruct((ROWS, D), BF16),
+            jax.ShapeDtypeStruct((ROWS, D), BF16),
+            jax.ShapeDtypeStruct((8, D), F32),
+            jax.ShapeDtypeStruct((FF // FSDP, D), BF16),
+            jax.ShapeDtypeStruct((D, FF // FSDP), BF16),
+            jax.ShapeDtypeStruct((D, 3 * D // FSDP), BF16),
+            jax.ShapeDtypeStruct((D, D // FSDP), BF16),
+        ),
+        in_specs=[sme, sme, sme] + [vm] * 8 + [hbm] * 4,
+        out_specs=(vm, vm, vm, hbm, hbm, hbm, hbm),
+        scratch_shapes=scratch,
+        compiler_params=pltpu.CompilerParams(
+            collective_id=0, has_side_effects=True, vmem_limit_bytes=63 * 2**20
+        ),
+    )(
+        holders,
+        halves,
+        order,
+        vec,
+        upb,
+        cos_tab,
+        sin_tab,
+        scos,
+        ssin,
+        tokens,
+        cotangent,
+        qkv_weight,
+        out_weight,
+        up_weight,
+        down_weight,
+    )
+    half = D // FSDP
+    return (
+        mixed,
+        tokens_grad,
+        lax.dynamic_slice(small[3], (f * half,), (half,)),
+        lax.dynamic_slice(small[4], (f * half,), (half,)),
+        qkv.astype(F32),
+        out_t.astype(F32).T,
+        up.astype(F32),
+        small[0:2].reshape(-1),
+        dn.astype(F32),
+        lax.dynamic_slice(small[2], (f * half,), (half,)),
+    )
+
+
 def solution(mesh):
     in_specs = (
         P(("fsdp", "ctx"), None),
@@ -446,6 +1444,7 @@
         P("fsdp", None),
         P("fsdp"),
     )
+    plan = fused_device if fits(mesh) else per_device
     return jax.shard_map(
-        per_device, mesh=mesh, in_specs=in_specs, out_specs=out_specs, check_vma=False
-    )
+        plan, mesh=mesh, in_specs=in_specs, out_specs=out_specs, check_vma=False
+    )

time: 1730 us -> 347 us (0.20)
  waiting for transfers between devices: 723 us -> 0 us
  blocking collectives: 549 us -> 0 us
  Pallas kernels: 0 us -> 308 us
  matrix products: 257 us -> 0 us
  local copies, waits for them, and re-layouts: 115 us -> 11.7 us
  other arithmetic: 52.1 us -> 21.4 us
    psum x1 -> x0, blocking collectives: 531 us -> none  [per_device(): lax.psum((share_gain, share_shift, share_qkv, share_out, share_up, share_...]
    reduce_scatter x5 -> x0, waiting for transfers between devices: 492 us -> none  [the longest x1 228 us: per_device(): lax.psum_scatter(blocks_out.reshape(seq_rows * lax.axis_size('ctx'), seq_...]
    pallas_call x0 -> x1, Pallas kernels: none -> 308 us  [fused_device(): pl.pallas_call(fused_kernel, out_shape=(jax.ShapeDtypeStruct((ROWS, D), B...]
    dot_general x28 -> x0, matrix products: 257 us -> none  [the longest x4 41.9 us: grad_scores(): jnp.einsum('qshe,kshe->shqk', query_rows, key_rows, preferred_element_typ...]
    all_gather x6 -> x0, waiting for transfers between devices: 229 us -> none  [the longest x1 75.3 us: per_device(): piece_keys = lax.all_gather(key_rows, 'ctx', axis=0, tiled=True)]
    dynamic_update_slice x4 -> x0, local copies, waits for them, and re-layouts: 56.4 us -> none  [per_device(): lax.scan(key_step, jnp.zeros((), jnp.float32), (split_groups(piece_keys,...]
    broadcast_in_dim x3 -> x0, other arithmetic: 23.6 us -> none  [per_device(): lax.scan(key_step, jnp.zeros((), jnp.float32), (split_groups(piece_keys,...]
    reduce_sum x14 -> x1, other arithmetic: 22.7 us -> 0.11 us  [fused_device(): jnp.sum(jnp.where(hits, jnp.arange(4 * CHIPS, dtype=jnp.int32)[None, :],...]
  transfers between devices with their start and end apart: 11 -> 0, of which waited for: 9 -> 0; matrix products, arithmetic and copies ran while one was open for 24% -> 0% of each run, Pallas kernels for 0% -> 0%
where the time goes in v1:
time: 347 us; the launch traced here: 342 us
  Pallas kernels  308 us (89%)
  other arithmetic  21.4 us (6%)
  local copies, waits for them, and re-layouts  11.7 us (3%)
    pallas_call x1, Pallas kernels, fused_device(): pl.pallas_call(fused_kernel, out_shape=(jax.ShapeDtypeStruct((ROWS, D), B...  308 us

profile of v1, /device:TPU:9, one launch (start us, length us, event | category | flops | bytes accessed | tf_op | source)
XLA Modules:
  0.0 342.3 jit_solution(12127982390395872719)
XLA Ops:
  0.7 0.7 broadcast_subtract_fusion
  1.6 0.3 fusion.6
  2.0 0.8 copy.28.cos_ref
  2.8 0.8 copy.29.sin_ref
  3.6 0.7 dynamic_slice.21
  4.3 0.6 broadcast_in_dim.123.upb_ref
  4.9 3.8 %fusion.3 = (f32[2048,64]{1,0:T(8,128)S(1)}, f32[2048,64]{1,0:T(8,128)S(1)}) fusion(f32[64]{0:T(128)S(1)} %get-tuple-element.65, f32[64]{0:T(128)S(1)} %get-tuple-element.66, f32[2048]{0:T(1024)S(1)} %iota_convert_fusion, pred[64]{0:T(512)(128)(4,1)S(1)} %iota_compare_fusion.2), kind=kLoop, calls=%fused_computation.6 | loop fusion | flops 655360 | bytes 1057344 | tf_op jit(solution)/shard_map/neg | solution.py:1297
  8.7 1.3 concatenate.10.scos_ref
  10.0 1.3 concatenate.11.ssin_ref
  11.5 0.1 select_reduce_fusion
  11.6 0.5 and_select_fusion.3
  12.3 0.7 maximum_maximum_fusion.vec_ref
  13.0 308.4 %shard_map.186 = (bf16[256,1024]{1,0:T(8,128)(2,1)}, bf16[256,1024]{1,0:T(8,128)(2,1)}, f32[8,1024]{1,0:T(8,128)}, bf16[2048,1024]{1,0:T(8,128)(2,1)}, bf16[1024...) custom-call(s32[32]{0:T(128)} %get-tuple-element.64.places_ref, ...), custom_call_target="tpu_custom_call" | custom-call | tf_op jit(solution)/shard_map/pallas_call | solution.py:1372
  321.4 6.8 %convert_element_type.46 = f32[1024,2048]{1,0:T(8,128)} convert(bf16[1024,2048]{1,0:T(8,128)(2,1)} %get-tuple-element.22) | non-fusion elementwise | flops 2097152 | bytes 12582912 | tf_op jit(solution)/shard_map/convert_element_type | solution.py:1414
  328.2 4.4 %convert_element_type.47 = f32[2048,1024]{1,0:T(8,128)} convert(bf16[2048,1024]{1,0:T(8,128)(2,1)S(1)} %copy-done) | non-fusion elementwise | flops 2097152 | bytes 12582912 | tf_op jit(solution)/shard_map/convert_element_type | solution.py:1416
  332.6 3.6 %convert_element_type.45 = f32[1024,1536]{1,0:T(8,128)} convert(bf16[1024,1536]{1,0:T(8,128)(2,1)S(1)} %copy-done.1) | non-fusion elementwise | flops 1572864 | bytes 9437184 | tf_op jit(solution)/shard_map/convert_element_type | solution.py:1412
  336.2 0.3 convert_bitcast_fusion
  336.5 1.8 copy.30
  338.4 0.6 constant_dynamic-slice_fusion.2
  338.9 0.6 constant_dynamic-slice_fusion.1
  339.5 0.6 constant_dynamic-slice_fusion
  340.1 0.6 copy.33
  340.7 0.8 copy.36
  341.5 0.8 copy.37
  (43 shorter events, 0.6 us)
Async XLA Ops:
  0.6 10.7 %copy-start.7 = (s32[16]{0:T(128)S(1)}, s32[16]{0:T(128)}, u32[]{:S(2)}) copy-start(s32[16]{0:T(128)} %param.12) | copy-start | bytes 196
  0.7 11.5 %copy-start.8 = (bf16[512]{0:T(512)(128)(2,1)S(1)}, bf16[512]{0:T(512)(128)(2,1)}, u32[]{:S(2)}) copy-start(bf16[512]{0:T(512)(128)(2,1)} %param.13) | copy-start | bytes 3076
  0.7 11.5 %copy-start.9 = (bf16[512]{0:T(512)(128)(2,1)S(1)}, bf16[512]{0:T(512)(128)(2,1)}, u32[]{:S(2)}) copy-start(bf16[512]{0:T(512)(128)(2,1)} %param.14) | copy-start | bytes 3076
  0.7 11.5 %copy-start.10 = (bf16[512]{0:T(512)(128)(2,1)S(1)}, bf16[512]{0:T(512)(128)(2,1)}, u32[]{:S(2)}) copy-start(bf16[512]{0:T(512)(128)(2,1)} %param.20) | copy-start | bytes 3076
  11.5 1.5 copy-start.6
  321.4 6.8 %copy-start = (bf16[2048,1024]{1,0:T(8,128)(2,1)S(1)}, bf16[2048,1024]{1,0:T(8,128)(2,1)}, u32[]{:S(2)}) copy-start(bf16[2048,1024]{1,0:T(8,128)(2,1)} %get-tuple-element.23) | copy-start | bytes 12582916
  328.2 4.4 %copy-start.1 = (bf16[1024,1536]{1,0:T(8,128)(2,1)S(1)}, bf16[1024,1536]{1,0:T(8,128)(2,1)}, u32[]{:S(2)}) copy-start(bf16[1024,1536]{1,0:T(8,128)(2,1)} %get-tuple-element.20) | copy-start | bytes 9437188
  332.6 3.6 %copy-start.2 = (bf16[1024,512]{1,0:T(8,128)(2,1)S(1)}, bf16[1024,512]{1,0:T(8,128)(2,1)}, u32[]{:S(2)}) copy-start(bf16[1024,512]{1,0:T(8,128)(2,1)} %get-tuple-element.21) | copy-start | bytes 3145732
  336.2 2.1 copy-start.5
  336.2 4.5 %copy-start.4 = (bf16[256,1024]{1,0:T(8,128)(2,1)S(1)}, bf16[256,1024]{1,0:T(8,128)(2,1)}, u32[]{:S(2)}) copy-start(bf16[256,1024]{1,0:T(8,128)(2,1)} %get-tuple-element.77) | copy-start | bytes 1572868
  336.2 5.3 %copy-start.3 = (bf16[256,1024]{1,0:T(8,128)(2,1)S(1)}, bf16[256,1024]{1,0:T(8,128)(2,1)}, u32[]{:S(2)}) copy-start(bf16[256,1024]{1,0:T(8,128)(2,1)} %get-tuple-element.78) | copy-start | bytes 1572868
